TPU v7x, 32 devices: a whole 2x2x4 slice. The times are simulated.
32 devices in a mesh: rooms: 2 (over y), gx: 4 (over z), gy: 2 (over x), gz: 2 (over core).
Axes of the slice: x: 2, y: 2, z: 4, core: 2. Of those that a mesh axis runs over, the one named last changes fastest.
Arguments:
- pressure_prior: float32 [16, 64, 512], P(('rooms', 'gx'), 'gy', 'gz'), parts along dimension 0, may hold values from -6 to 6
- pressure_now: float32 [16, 64, 512], P(('rooms', 'gx'), 'gy', 'gz'), parts along dimension 0, may hold values from -6 to 6
- adjoint_end: float32 [16, 64, 512], P(('rooms', 'gx'), 'gy', 'gz'), parts along dimension 0, may hold values from -6 to 6
- adjoint_near: float32 [16, 64, 512], P(('rooms', 'gx'), 'gy', 'gz'), parts along dimension 0, may hold values from -6 to 6
- wall_faces: int32 [16, 64, 512], P(('rooms', 'gx'), 'gy', 'gz'), parts along dimension 0, may hold values from 0 to 3
- material_ids: int32 [16, 64, 512], P(('rooms', 'gx'), 'gy', 'gz'), parts along dimension 0, may hold values from 0 to 63
- admittance: float32 [64], replicated, may hold values from 0.05 to 0.6
- receivers: int32 [128, 3], P('rooms'), parts along dimension 0, may hold values from 0 to 511, as said below
- targets: float32 [128, 2], P('rooms'), parts along dimension 0, may hold values from -6 to 6
Outputs:
- adjoint_prior: float32 [16, 64, 512], P(('rooms', 'gx'), 'gy', 'gz'), parts along dimension 0
- adjoint_now: float32 [16, 64, 512], P(('rooms', 'gx'), 'gy', 'gz'), parts along dimension 0
- grad_admittance: float32 [128], P('rooms'), parts along dimension 0
There are 2 independent parts, one for each index of `rooms`. A program takes and returns all parts, laid end to end along the dimension named above; an argument that names none is the same for every part. Nothing has to cross between parts.
Inputs may be any that keep to these rules, and one draw needn't show every extreme that they name: `receivers`: column 0 is below 8, column 1 below 64, column 2 below 512.
All inputs are finite; a program needn't handle non-finite values.
Results may differ from a plain program's by a relative error of at most 0.00015.
Values sent between devices are 32-bit elements; how exact they have to be, the bound alone decides.
A program may use at most 64 MiB of HBM per device.

v0:
```python
import math

import jax
import jax.numpy as jnp
from jax import lax
from jax.sharding import PartitionSpec as P


def padded_2(cells, sides, width):
    for axis, dim in sides:
        count = lax.axis_size(axis)
        ends = count - 1
        head = lax.slice_in_dim(cells, 0, width, axis=dim)
        tail = lax.slice_in_dim(cells, cells.shape[dim] - width, cells.shape[dim], axis=dim)
        cells = jnp.concatenate(
            [
                lax.ppermute(tail, axis, [(i, (i + 1) % count) for i in range(ends)]),
                cells,
                lax.ppermute(head, axis, [((i + 1) % count, i) for i in range(ends)]),
            ],
            axis=dim,
        )
    return cells


def stencil(padded):
    centre = padded[1:-1, 1:-1, 1:-1]
    beside_all = padded[2:, 1:-1, 1:-1] + padded[:-2, 1:-1, 1:-1]
    beside_all = beside_all + padded[1:-1, 2:, 1:-1] + padded[1:-1, :-2, 1:-1]
    beside_all = beside_all + padded[1:-1, 1:-1, 2:] + padded[1:-1, 1:-1, :-2]
    return beside_all - 6.0 * centre


def pressure_laplace(field):
    padded = padded_2(field, (("gx", 0), ("gy", 1), ("gz", 2)), 1)
    return stencil(padded)


def adjoint_laplace(field):
    padded = padded_2(field, (("gx", 0), ("gy", 1), ("gz", 2)), 1)
    return stencil(padded)


def per_material(terms, material_ids, kinds):
    return jax.ops.segment_sum(terms.reshape(-1), material_ids.reshape(-1), num_segments=kinds)


def step_total(terms, material_ids, kinds):
    return lax.psum(per_material(terms, material_ids, kinds), ("gx", "gy", "gz"))


def local(
    pressure_prior,
    pressure_now,
    adjoint_end,
    adjoint_near,
    wall_faces,
    material_ids,
    admittance,
    receivers,
    targets,
):
    span_x, span_y, span_z = pressure_now.shape
    kinds = admittance.shape[0]
    wall_count = wall_faces.astype(jnp.float32)
    loss_rate = 0.5 * wall_count * admittance[material_ids]
    inverse_loss = 1.0 / (1.0 + loss_rate)
    reflect = 2.0 * inverse_loss - 1.0
    pressure_two = (
        inverse_loss * (2.0 * pressure_now + 0.25 * pressure_laplace(pressure_now))
        - reflect * pressure_prior
    )
    pressure_three = (
        inverse_loss * (2.0 * pressure_two + 0.25 * pressure_laplace(pressure_two))
        - reflect * pressure_now
    )
    offsets = jnp.stack(
        [
            lax.axis_index("gx") * span_x,
            lax.axis_index("gy") * span_y,
            lax.axis_index("gz") * span_z,
        ]
    )
    relative = receivers - offsets[None, :]
    limits = jnp.array([span_x, span_y, span_z], dtype=jnp.int32)
    inside = jnp.all((relative >= 0) & (relative < limits[None, :]), axis=1)
    position = jnp.where(
        inside, (relative[:, 0] * span_y + relative[:, 1]) * span_z + relative[:, 2], 0
    )

    def misfit(field, column):
        values = field.reshape(-1)[position]
        mismatch = jnp.where(inside, values - targets[:, column], 0.0)
        return jnp.zeros((field.size,), jnp.float32).at[position].add(mismatch).reshape(field.shape)

    adjoint_three = adjoint_end + misfit(pressure_three, 1)
    incoming_two = adjoint_near + misfit(pressure_two, 0)
    weighted_three = inverse_loss * adjoint_three
    adjoint_two = incoming_two + 2.0 * weighted_three + 0.25 * adjoint_laplace(weighted_three)
    weighted_two = inverse_loss * adjoint_two
    adjoint_now = (
        -reflect * adjoint_three + 2.0 * weighted_two + 0.25 * adjoint_laplace(weighted_two)
    )
    adjoint_prior = -reflect * adjoint_two
    term_three = 0.5 * wall_count * weighted_three * (pressure_now - pressure_three)
    term_two = 0.5 * wall_count * weighted_two * (pressure_prior - pressure_two)
    cell_total = pressure_now.size * lax.axis_size("gx") * lax.axis_size("gy") * lax.axis_size("gz")
    scaling = 16.0 / math.sqrt(cell_total)
    summed = step_total(term_three, material_ids, kinds) + step_total(term_two, material_ids, kinds)
    return (adjoint_prior, adjoint_now, scaling * summed)


def solution(mesh):
    in_specs = (
        P(("rooms", "gx"), "gy", "gz"),
        P(("rooms", "gx"), "gy", "gz"),
        P(("rooms", "gx"), "gy", "gz"),
        P(("rooms", "gx"), "gy", "gz"),
        P(("rooms", "gx"), "gy", "gz"),
        P(("rooms", "gx"), "gy", "gz"),
        P(),
        P("rooms", None),
        P("rooms", None),
    )
    out_specs = (P(("rooms", "gx"), "gy", "gz"), P(("rooms", "gx"), "gy", "gz"), P("rooms"))
    return jax.shard_map(local, mesh=mesh, in_specs=in_specs, out_specs=out_specs, check_vma=False)
```

profile of v0, /device:TPU:0, one launch (start us, length us, event | category | flops | bytes accessed | tf_op | source)
XLA Modules:
  0.0 441.7 jit_solution(16045432210676245795)
XLA Ops:
  1.5 4.9 %collective-permute-start.1 = (f32[1,32,256]{2,1,0:T(8,128)S(1)}, f32[1,32,256]{2,1,0:T(8,128)S(1)}, u32[]{:S(2)}, u32[]{:S(2)}) collective-permute-start(f32[1,32,256]{2,1,0:T(8,128)S(1)} %get-tuple-element.35), channel_id=1, source_target_pairs={{0,4},{4,8},{8,12},{1,5},{5,9},{9,13},{2,6},{6,10},{10,14},{3,7},{... | collective-permute-start | bytes 98312 | tf_op jit(solution)/shard_map/ppermute | solution.py:17
  6.4 1.3 collective-permute-start
  8.6 3.6 collective-permute-done
  12.2 1.3 collective-permute-start.2
  13.5 4.5 %collective-permute-start.3 = (f32[4,1,256]{2,1,0:T(1,128)S(1)}, f32[4,1,256]{2,1,0:T(1,128)S(1)}, u32[]{:S(2)}, u32[]{:S(2)}) collective-permute-start(f32[4,1,256]{2,1,0:T(1,128)S(1)} %get-tuple-element.26), channel_id=1, source_target_pairs={{0,2},{1,3},{4,6},{5,7},{8,10},{9,11},{12,14},{13,15},{16,18},{17,... | collective-permute-start | bytes 12296 | tf_op jit(solution)/shard_map/ppermute | solution.py:17
  19.5 1.3 collective-permute-start.4
  20.8 3.0 collective-permute-start.5
  23.9 97.2 %gather_fusion = f32[16384]{0:T(1024)S(1)} fusion(f32[64]{0:T(128)S(1)} %copy-done, s32[16384]{0:T(1024)S(1)} %broadcast_clamp_fusion), kind=kCustom, calls=%fused_computation | custom fusion | bytes 196608 | tf_op jit(solution)/shard_map/gather | solution.py:66
  122.2 1.3 collective-permute-start.6
  123.5 4.5 %collective-permute-start.7 = (f32[1,32,256]{2,1,0:T(8,128)S(1)}, f32[1,32,256]{2,1,0:T(8,128)S(1)}, u32[]{:S(2)}, u32[]{:S(2)}) collective-permute-start(f32[1,32,256]{2,1,0:T(8,128)S(1)} %get-tuple-element.32), channel_id=1, source_target_pairs={{0,4},{4,8},{8,12},{1,5},{5,9},{9,13},{2,6},{6,10},{10,14},{3,7},{... | collective-permute-start | bytes 98312 | tf_op jit(solution)/shard_map/ppermute | solution.py:17
  128.1 1.5 collective-permute-done.7
  129.6 1.3 collective-permute-start.8
  130.9 4.5 %collective-permute-start.9 = (f32[4,1,256]{2,1,0:T(1,128)S(1)}, f32[4,1,256]{2,1,0:T(1,128)S(1)}, u32[]{:S(2)}, u32[]{:S(2)}) collective-permute-start(f32[4,1,256]{2,1,0:T(1,128)S(1)} %get-tuple-element.24), channel_id=1, source_target_pairs={{0,2},{1,3},{4,6},{5,7},{8,10},{9,11},{12,14},{13,15},{16,18},{17,... | collective-permute-start | bytes 12296 | tf_op jit(solution)/shard_map/ppermute | solution.py:17
  135.5 1.3 collective-permute-done.9
  136.9 1.3 collective-permute-start.10
  138.2 3.0 collective-permute-start.11
  145.0 1.3 collective-permute-start.12
  146.3 4.9 %collective-permute-start.13 = (f32[1,32,256]{2,1,0:T(8,128)S(1)}, f32[1,32,256]{2,1,0:T(8,128)S(1)}, u32[]{:S(2)}, u32[]{:S(2)}) collective-permute-start(f32[1,32,256]{2,1,0:T(8,128)S(1)} %get-tuple-element.30), channel_id=1, source_target_pairs={{0,4},{4,8},{8,12},{1,5},{5,9},{9,13},{2,6},{6,10},{10,14},{3,7},{... | collective-permute-start | bytes 98312 | tf_op jit(solution)/shard_map/ppermute | solution.py:17
  151.2 1.6 collective-permute-done.13
  154.1 4.5 %collective-permute-start.15 = (f32[4,1,256]{2,1,0:T(1,128)S(1)}, f32[4,1,256]{2,1,0:T(1,128)S(1)}, u32[]{:S(2)}, u32[]{:S(2)}) collective-permute-start(f32[4,1,256]{2,1,0:T(1,128)S(1)} %get-tuple-element.22), channel_id=1, source_target_pairs={{0,2},{1,3},{4,6},{5,7},{8,10},{9,11},{12,14},{13,15},{16,18},{17,... | collective-permute-start | bytes 12296 | tf_op jit(solution)/shard_map/ppermute | solution.py:17
  158.6 1.3 collective-permute-done.15
  160.0 1.3 collective-permute-start.16
  161.3 3.0 collective-permute-start.17
  166.4 1.3 collective-permute-start.18
  167.7 4.9 %collective-permute-start.19 = (f32[1,32,256]{2,1,0:T(8,128)S(1)}, f32[1,32,256]{2,1,0:T(8,128)S(1)}, u32[]{:S(2)}, u32[]{:S(2)}) collective-permute-start(f32[1,32,256]{2,1,0:T(8,128)S(1)} %get-tuple-element.28), channel_id=1, source_target_pairs={{0,4},{4,8},{8,12},{1,5},{5,9},{9,13},{2,6},{6,10},{10,14},{3,7},{... | collective-permute-start | bytes 98312 | tf_op jit(solution)/shard_map/ppermute | solution.py:17
  172.7 113.4 %scatter_custom_fusion.2 = f32[64]{0:T(128)S(1)} fusion(s32[16384]{0:T(1024)S(1)} %bitcast.40, f32[16384]{0:T(1024)S(1)} %bitcast.43, f32[]{:T(128)} %constant.7.clone.1), kind=kCustom, calls=%fused_computation.151 | custom fusion | flops 16384 | bytes 260 | tf_op jit(solution)/shard_map/scatter-add | solution.py:45
  286.1 1.3 collective-permute-start.20
  287.4 4.5 %collective-permute-start.21 = (f32[4,1,256]{2,1,0:T(1,128)S(1)}, f32[4,1,256]{2,1,0:T(1,128)S(1)}, u32[]{:S(2)}, u32[]{:S(2)}) collective-permute-start(f32[4,1,256]{2,1,0:T(1,128)S(1)} %get-tuple-element.20), channel_id=1, source_target_pairs={{0,2},{1,3},{4,6},{5,7},{8,10},{9,11},{12,14},{13,15},{16,18},{17,... | collective-permute-start | bytes 12296 | tf_op jit(solution)/shard_map/ppermute | solution.py:17
  292.7 113.4 %scatter_custom_fusion.3 = f32[64]{0:T(128)S(1)} fusion(s32[16384]{0:T(1024)S(1)} %bitcast.41, f32[16384]{0:T(1024)S(1)} %bitcast.42, f32[]{:T(128)} %constant.7.clone.1), kind=kCustom, calls=%fused_computation.149 | custom fusion | flops 16384 | bytes 260 | tf_op jit(solution)/shard_map/scatter-add | solution.py:45
  406.1 29.5 %psum.16 = f32[64]{0:T(128)S(1)} all-reduce(f32[64]{0:T(128)S(1)} %add.158), channel_id=1, replica_groups=mesh['rooms'=2,'gx'=4,'gy'=2,'gz'=2] {'gx','gy','gz'}, use_global_device_ids=true, to_apply=%region_4.5 | all-reduce | flops 64 | bytes 512 | tf_op jit(solution)/shard_map/psum | solution.py:49
  435.7 1.3 collective-permute-start.22
  437.0 3.0 collective-permute-start.23
  (87 shorter events, 14.0 us)
Async XLA Ops:
  0.6 23.3 %copy-start = (f32[64]{0:T(128)S(1)}, f32[64]{0:T(128)}, u32[]{:S(2)}) copy-start(f32[64]{0:T(128)} %param.16) | copy-start | bytes 772
  0.6 7.1 %copy-start.4 = (s32[2,32,256]{2,1,0:T(8,128)S(1)}, s32[2,32,256]{2,1,0:T(8,128)}, u32[]{:S(2)}) copy-start(s32[2,32,256]{2,1,0:T(8,128)} %param.15) | copy-start | bytes 196612
  1.5 6.5 %collective-permute-start.1 = (f32[1,32,256]{2,1,0:T(8,128)S(1)}, f32[1,32,256]{2,1,0:T(8,128)S(1)}, u32[]{:S(2)}, u32[]{:S(2)}) collective-permute-start(f32[1,32,256]{2,1,0:T(8,128)S(1)} %get-tuple-element.35), channel_id=1, source_target_pairs={{0,4},{4,8},{8,12},{1,5},{5,9},{9,13},{2,6},{6,10},{10,14},{3,7},{... | collective-permute-start | bytes 98312 | tf_op jit(solution)/shard_map/ppermute | solution.py:17
  6.4 5.8 %collective-permute-start = (f32[1,32,256]{2,1,0:T(8,128)S(1)}, f32[1,32,256]{2,1,0:T(8,128)S(1)}, u32[]{:S(2)}, u32[]{:S(2)}) collective-permute-start(f32[1,32,256]{2,1,0:T(8,128)S(1)} %get-tuple-element.34), channel_id=1, source_target_pairs={{4,0},{8,4},{12,8},{5,1},{9,5},{13,9},{6,2},{10,6},{14,10},{7,3},{... | collective-permute-start | bytes 98312 | tf_op jit(solution)/shard_map/ppermute | solution.py:19
  7.8 0.8 copy-start.1
  12.2 5.9 %collective-permute-start.2 = (f32[4,1,256]{2,1,0:T(1,128)S(1)}, f32[4,1,256]{2,1,0:T(1,128)S(1)}, u32[]{:S(2)}, u32[]{:S(2)}) collective-permute-start(f32[4,1,256]{2,1,0:T(1,128)S(1)} %get-tuple-element.27), channel_id=1, source_target_pairs={{2,0},{3,1},{6,4},{7,5},{10,8},{11,9},{14,12},{15,13},{18,16},{19,... | collective-permute-start | bytes 12296 | tf_op jit(solution)/shard_map/ppermute | solution.py:19
  13.5 5.9 %collective-permute-start.3 = (f32[4,1,256]{2,1,0:T(1,128)S(1)}, f32[4,1,256]{2,1,0:T(1,128)S(1)}, u32[]{:S(2)}, u32[]{:S(2)}) collective-permute-start(f32[4,1,256]{2,1,0:T(1,128)S(1)} %get-tuple-element.26), channel_id=1, source_target_pairs={{0,2},{1,3},{4,6},{5,7},{8,10},{9,11},{12,14},{13,15},{16,18},{17,... | collective-permute-start | bytes 12296 | tf_op jit(solution)/shard_map/ppermute | solution.py:17
  19.5 101.7 %collective-permute-start.4 = (f32[4,34,1]{2,1,0:T(8,128)S(1)}, f32[4,34,1]{2,1,0:T(8,128)S(1)}, u32[]{:S(2)}, u32[]{:S(2)}) collective-permute-start(f32[4,34,1]{2,1,0:T(8,128)S(1)} %get-tuple-element.18), channel_id=1, source_target_pairs={{1,0},{3,2},{5,4},{7,6},{9,8},{11,10},{13,12},{15,14},{17,16},{19,... | collective-permute-start | bytes 1640 | tf_op jit(solution)/shard_map/ppermute | solution.py:19
  20.8 100.4 %collective-permute-start.5 = (f32[4,34,1]{2,1,0:T(8,128)S(1)}, f32[4,34,1]{2,1,0:T(8,128)S(1)}, u32[]{:S(2)}, u32[]{:S(2)}) collective-permute-start(f32[4,34,1]{2,1,0:T(8,128)S(1)} %get-tuple-element.19), channel_id=1, source_target_pairs={{0,1},{2,3},{4,5},{6,7},{8,9},{10,11},{12,13},{14,15},{16,17},{18,... | collective-permute-start | bytes 1640 | tf_op jit(solution)/shard_map/ppermute | solution.py:17
  121.1 0.9 copy-start.3
  122.1 5.9 %copy-start.7 = (s32[64,3]{0,1:T(4,128)S(1)}, s32[64,3]{0,1:T(4,128)}, u32[]{:S(2)}) copy-start(s32[64,3]{0,1:T(4,128)} %param.17) | copy-start | bytes 2308
  122.2 5.9 %copy-start.9 = (s32[3]{0:T(128)S(1)}, s32[3]{0:T(128)}, u32[]{:S(2)}) copy-start(s32[3]{0:T(128)} %constant.50.clone) | copy-start | bytes 40
  122.2 6.0 %collective-permute-start.6 = (f32[1,32,256]{2,1,0:T(8,128)S(1)}, f32[1,32,256]{2,1,0:T(8,128)S(1)}, u32[]{:S(2)}, u32[]{:S(2)}) collective-permute-start(f32[1,32,256]{2,1,0:T(8,128)S(1)} %get-tuple-element.33), channel_id=1, source_target_pairs={{4,0},{8,4},{12,8},{5,1},{9,5},{13,9},{6,2},{10,6},{14,10},{7,3},{... | collective-permute-start | bytes 98312 | tf_op jit(solution)/shard_map/ppermute | solution.py:19
  123.5 6.1 %collective-permute-start.7 = (f32[1,32,256]{2,1,0:T(8,128)S(1)}, f32[1,32,256]{2,1,0:T(8,128)S(1)}, u32[]{:S(2)}, u32[]{:S(2)}) collective-permute-start(f32[1,32,256]{2,1,0:T(8,128)S(1)} %get-tuple-element.32), channel_id=1, source_target_pairs={{0,4},{4,8},{8,12},{1,5},{5,9},{9,13},{2,6},{6,10},{10,14},{3,7},{... | collective-permute-start | bytes 98312 | tf_op jit(solution)/shard_map/ppermute | solution.py:17
  129.6 5.9 %collective-permute-start.8 = (f32[4,1,256]{2,1,0:T(1,128)S(1)}, f32[4,1,256]{2,1,0:T(1,128)S(1)}, u32[]{:S(2)}, u32[]{:S(2)}) collective-permute-start(f32[4,1,256]{2,1,0:T(1,128)S(1)} %get-tuple-element.25), channel_id=1, source_target_pairs={{2,0},{3,1},{6,4},{7,5},{10,8},{11,9},{14,12},{15,13},{18,16},{19,... | collective-permute-start | bytes 12296 | tf_op jit(solution)/shard_map/ppermute | solution.py:19
  130.9 5.9 %collective-permute-start.9 = (f32[4,1,256]{2,1,0:T(1,128)S(1)}, f32[4,1,256]{2,1,0:T(1,128)S(1)}, u32[]{:S(2)}, u32[]{:S(2)}) collective-permute-start(f32[4,1,256]{2,1,0:T(1,128)S(1)} %get-tuple-element.24), channel_id=1, source_target_pairs={{0,2},{1,3},{4,6},{5,7},{8,10},{9,11},{12,14},{13,15},{16,18},{17,... | collective-permute-start | bytes 12296 | tf_op jit(solution)/shard_map/ppermute | solution.py:17
  136.9 5.2 %collective-permute-start.10 = (f32[4,34,1]{2,1,0:T(8,128)S(1)}, f32[4,34,1]{2,1,0:T(8,128)S(1)}, u32[]{:S(2)}, u32[]{:S(2)}) collective-permute-start(f32[4,34,1]{2,1,0:T(8,128)S(1)} %get-tuple-element.16), channel_id=1, source_target_pairs={{1,0},{3,2},{5,4},{7,6},{9,8},{11,10},{13,12},{15,14},{17,16},{19,... | collective-permute-start | bytes 1640 | tf_op jit(solution)/shard_map/ppermute | solution.py:19
  138.2 3.9 collective-permute-start.11
  144.1 0.8 copy-start.5
  145.0 6.2 %collective-permute-start.12 = (f32[1,32,256]{2,1,0:T(8,128)S(1)}, f32[1,32,256]{2,1,0:T(8,128)S(1)}, u32[]{:S(2)}, u32[]{:S(2)}) collective-permute-start(f32[1,32,256]{2,1,0:T(8,128)S(1)} %get-tuple-element.31), channel_id=1, source_target_pairs={{4,0},{8,4},{12,8},{5,1},{9,5},{13,9},{6,2},{10,6},{14,10},{7,3},{... | collective-permute-start | bytes 98312 | tf_op jit(solution)/shard_map/ppermute | solution.py:19
  146.3 6.5 %collective-permute-start.13 = (f32[1,32,256]{2,1,0:T(8,128)S(1)}, f32[1,32,256]{2,1,0:T(8,128)S(1)}, u32[]{:S(2)}, u32[]{:S(2)}) collective-permute-start(f32[1,32,256]{2,1,0:T(8,128)S(1)} %get-tuple-element.30), channel_id=1, source_target_pairs={{0,4},{4,8},{8,12},{1,5},{5,9},{9,13},{2,6},{6,10},{10,14},{3,7},{... | collective-permute-start | bytes 98312 | tf_op jit(solution)/shard_map/ppermute | solution.py:17
  152.8 5.8 %collective-permute-start.14 = (f32[4,1,256]{2,1,0:T(1,128)S(1)}, f32[4,1,256]{2,1,0:T(1,128)S(1)}, u32[]{:S(2)}, u32[]{:S(2)}) collective-permute-start(f32[4,1,256]{2,1,0:T(1,128)S(1)} %get-tuple-element.23), channel_id=1, source_target_pairs={{2,0},{3,1},{6,4},{7,5},{10,8},{11,9},{14,12},{15,13},{18,16},{19,... | collective-permute-start | bytes 12296 | tf_op jit(solution)/shard_map/ppermute | solution.py:19
  154.1 5.9 %collective-permute-start.15 = (f32[4,1,256]{2,1,0:T(1,128)S(1)}, f32[4,1,256]{2,1,0:T(1,128)S(1)}, u32[]{:S(2)}, u32[]{:S(2)}) collective-permute-start(f32[4,1,256]{2,1,0:T(1,128)S(1)} %get-tuple-element.22), channel_id=1, source_target_pairs={{0,2},{1,3},{4,6},{5,7},{8,10},{9,11},{12,14},{13,15},{16,18},{17,... | collective-permute-start | bytes 12296 | tf_op jit(solution)/shard_map/ppermute | solution.py:17
  160.0 5.4 %collective-permute-start.16 = (f32[4,34,1]{2,1,0:T(8,128)S(1)}, f32[4,34,1]{2,1,0:T(8,128)S(1)}, u32[]{:S(2)}, u32[]{:S(2)}) collective-permute-start(f32[4,34,1]{2,1,0:T(8,128)S(1)} %get-tuple-element.14), channel_id=1, source_target_pairs={{1,0},{3,2},{5,4},{7,6},{9,8},{11,10},{13,12},{15,14},{17,16},{19,... | collective-permute-start | bytes 1640 | tf_op jit(solution)/shard_map/ppermute | solution.py:19
  161.3 4.1 collective-permute-start.17
  165.4 0.8 copy-start.6
  166.4 119.7 %collective-permute-start.18 = (f32[1,32,256]{2,1,0:T(8,128)S(1)}, f32[1,32,256]{2,1,0:T(8,128)S(1)}, u32[]{:S(2)}, u32[]{:S(2)}) collective-permute-start(f32[1,32,256]{2,1,0:T(8,128)S(1)} %get-tuple-element.29), channel_id=1, source_target_pairs={{4,0},{8,4},{12,8},{5,1},{9,5},{13,9},{6,2},{10,6},{14,10},{7,3},{... | collective-permute-start | bytes 98312 | tf_op jit(solution)/shard_map/ppermute | solution.py:19
  167.7 118.4 %collective-permute-start.19 = (f32[1,32,256]{2,1,0:T(8,128)S(1)}, f32[1,32,256]{2,1,0:T(8,128)S(1)}, u32[]{:S(2)}, u32[]{:S(2)}) collective-permute-start(f32[1,32,256]{2,1,0:T(8,128)S(1)} %get-tuple-element.28), channel_id=1, source_target_pairs={{0,4},{4,8},{8,12},{1,5},{5,9},{9,13},{2,6},{6,10},{10,14},{3,7},{... | collective-permute-start | bytes 98312 | tf_op jit(solution)/shard_map/ppermute | solution.py:17
  286.1 149.5 %collective-permute-start.20 = (f32[4,1,256]{2,1,0:T(1,128)S(1)}, f32[4,1,256]{2,1,0:T(1,128)S(1)}, u32[]{:S(2)}, u32[]{:S(2)}) collective-permute-start(f32[4,1,256]{2,1,0:T(1,128)S(1)} %get-tuple-element.21), channel_id=1, source_target_pairs={{2,0},{3,1},{6,4},{7,5},{10,8},{11,9},{14,12},{15,13},{18,16},{19,... | collective-permute-start | bytes 12296 | tf_op jit(solution)/shard_map/ppermute | solution.py:19
  287.4 148.2 %collective-permute-start.21 = (f32[4,1,256]{2,1,0:T(1,128)S(1)}, f32[4,1,256]{2,1,0:T(1,128)S(1)}, u32[]{:S(2)}, u32[]{:S(2)}) collective-permute-start(f32[4,1,256]{2,1,0:T(1,128)S(1)} %get-tuple-element.20), channel_id=1, source_target_pairs={{0,2},{1,3},{4,6},{5,7},{8,10},{9,11},{12,14},{13,15},{16,18},{17,... | collective-permute-start | bytes 12296 | tf_op jit(solution)/shard_map/ppermute | solution.py:17
  435.7 4.9 %collective-permute-start.22 = (f32[4,34,1]{2,1,0:T(8,128)S(1)}, f32[4,34,1]{2,1,0:T(8,128)S(1)}, u32[]{:S(2)}, u32[]{:S(2)}) collective-permute-start(f32[4,34,1]{2,1,0:T(8,128)S(1)} %get-tuple-element.12), channel_id=1, source_target_pairs={{1,0},{3,2},{5,4},{7,6},{9,8},{11,10},{13,12},{15,14},{17,16},{19,... | collective-permute-start | bytes 1640 | tf_op jit(solution)/shard_map/ppermute | solution.py:19
  437.0 3.9 collective-permute-start.23
  (2 other events, 1.6 us)
where the time goes:
time: 443 us; the launch traced here: 442 us
  other arithmetic  232 us (52%)
  local copies, waits for them, and re-layouts  103 us (23%)
  starting transfers between devices  65 us (15%)
  blocking collectives  29.5 us (7%)
  waiting for transfers between devices  11.2 us (3%)
    scatter-add x2, other arithmetic, per_material(): jax.ops.segment_sum(terms.reshape(-1), material_ids.reshape(-1), num_segm...  227 us
    gather x2, local copies, waits for them, and re-layouts, local(): loss_rate = 0.5 * wall_count * admittance[material_ids]  97.2 us
    ppermute x12, starting transfers between devices, padded_2(): lax.ppermute(tail, axis, [(i, (i + 1) % count) for i in range(ends)])  49.5 us
    psum x1, blocking collectives, step_total(): lax.psum(per_material(terms, material_ids, kinds), ('gx', 'gy', 'gz'))  29.5 us
    ppermute x12, starting transfers between devices, padded_2(): lax.ppermute(head, axis, [((i + 1) % count, i) for i in range(ends)])  15.5 us
  transfers between devices with their start and end apart: 24, of which 9 were waited for; matrix products, arithmetic and copies ran while one was open for 74% of the time, Pallas kernels for 0%

commit v1 on v0

v1 whole, which is shorter than its diff:
```python
import functools
import math

import jax
import jax.numpy as jnp
from jax import lax
from jax.experimental import pallas as pl
from jax.experimental.pallas import tpu as pltpu
from jax.sharding import PartitionSpec as P

HIGHEST = lax.Precision.HIGHEST
NOW, TWO, W3, W2 = range(4)


def kernel(
    sizes,
    scaling,
    now_in,
    prior_in,
    end_in,
    near_in,
    wall_in,
    ids_in,
    table_ref,
    receivers_ref,
    targets_ref,
    prior_out,
    now_out,
    grad_out,
    now_ref,
    prior_ref,
    end_ref,
    near_ref,
    wall_ref,
    ids_ref,
    field_ref,
    result_ref,
    bins_ref,
    slots_ref,
    hx,
    hy,
    hz,
    in_sems,
    out_sems,
    send_sems,
    recv_sems,
    sum_sems,
):
    nx, ny, nz = sizes
    count = nx * ny * nz
    ix, iy, iz = lax.axis_index("gx"), lax.axis_index("gy"), lax.axis_index("gz")
    me = (ix * ny + iy) * nz + iz
    span_x, span_y, span_z = now_ref.shape
    rows = span_x * span_y
    half = span_z // 2

    def peer(step):
        other = lax.rem(me + step, count)
        return {
            "gx": other // (ny * nz),
            "gy": lax.rem(other // nz, ny),
            "gz": lax.rem(other, nz),
        }

    loads = [
        pltpu.make_async_copy(source, target, in_sems.at[i])
        for i, (source, target) in enumerate(
            (
                (ids_in, ids_ref),
                (wall_in, wall_ref),
                (now_in, now_ref),
                (prior_in, prior_ref),
                (end_in, end_ref),
                (near_in, near_ref),
            )
        )
    ]
    for load in loads:
        load.start()

    barrier = pltpu.get_barrier_semaphore()

    @pl.loop(1, count)
    def _(step):
        pl.semaphore_signal(
            barrier, inc=1, device_id=peer(step), device_id_type=pl.DeviceIdType.MESH
        )

    pl.semaphore_wait(barrier, count - 1)

    def links(level, source):
        def copy(part, target, way, where):
            return pltpu.make_async_remote_copy(
                src_ref=part,
                dst_ref=target,
                send_sem=send_sems.at[level, way],
                recv_sem=recv_sems.at[level, way],
                device_id=where,
                device_id_type=pl.DeviceIdType.MESH,
            )

        last = span_x - 1
        return (
            (copy(source.at[last], hx.at[level, 0], 0, {"gx": ix + 1}), ix < nx - 1, ix > 0),
            (copy(source.at[0], hx.at[level, 1], 1, {"gx": ix - 1}), ix > 0, ix < nx - 1),
            (
                copy(source.at[:, pl.ds(span_y - 8, 8), :], hy.at[level, 0], 2, {"gy": iy + 1}),
                iy < ny - 1,
                iy > 0,
            ),
            (
                copy(source.at[:, pl.ds(0, 8), :], hy.at[level, 1], 3, {"gy": iy - 1}),
                iy > 0,
                iy < ny - 1,
            ),
            (
                copy(
                    source.at[:, :, pl.ds(pl.multiple_of((1 - iz) * half, half), half)],
                    hz.at[level],
                    4,
                    {"gz": 1 - iz},
                ),
                None,
                None,
            ),
        )

    def when(test, act):
        if test is None:
            act()
        else:
            pl.when(test)(act)

    def send(level, source):
        for copy, sends, _ in links(level, source):
            when(sends, copy.start)

    def receive(level, source):
        for copy, _, receives in links(level, source):
            when(receives, copy.wait_recv)

    def sent(level, source):
        for copy, sends, _ in links(level, source):
            when(sends, copy.wait_send)

    send(NOW, now_in)

    for test, buffer, side in (
        (ix == 0, hx, 0),
        (ix == nx - 1, hx, 1),
        (iy == 0, hy, 0),
        (iy == ny - 1, hy, 1),
    ):

        @pl.when(test)
        def _():
            for level in range(4):
                buffer[level, side] = jnp.zeros(buffer.shape[2:], jnp.float32)

    row = lax.broadcasted_iota(jnp.int32, (rows, span_z), 0)
    lane = lax.broadcasted_iota(jnp.int32, (rows, span_z), 1)
    top = lax.rem(row, span_y) == 0
    bottom = lax.rem(row, span_y) == span_y - 1

    def laplace(field, level):
        before_x = jnp.concatenate([hx[level, 0], field[: rows - span_y]], axis=0)
        after_x = jnp.concatenate([field[span_y:], hx[level, 1]], axis=0)
        shape = (span_x, span_y, span_z)
        before_y = jnp.broadcast_to(hy[level, 0][:, 7:8, :], shape).reshape(rows, span_z)
        after_y = jnp.broadcast_to(hy[level, 1][:, 0:1, :], shape).reshape(rows, span_z)
        before_y = jnp.where(top, before_y, pltpu.roll(field, 1, 0))
        after_y = jnp.where(bottom, after_y, pltpu.roll(field, rows - 1, 0))
        beside = hz[level].reshape(rows, half)
        before_z = jnp.where(iz == 1, beside[:, half - 1 :], 0.0)
        after_z = jnp.where(iz == 0, beside[:, :1], 0.0)
        before_z = jnp.where(lane == 0, before_z, pltpu.roll(field, 1, 1))
        after_z = jnp.where(lane == span_z - 1, after_z, pltpu.roll(field, span_z - 1, 1))
        total = before_x + after_x + before_y + after_y + before_z + after_z
        return total - 6.0 * field

    def flat(ref):
        return ref[...].reshape(rows, span_z)

    place = receivers_ref[...]
    at_x = place[:, 0:1] - ix * span_x
    at_y = place[:, 1:2] - iy * span_y
    at_z = place[:, 2:3] - iz * span_z
    inside = (at_x >= 0) & (at_x < span_x) & (at_y >= 0) & (at_y < span_y)
    inside = inside & (at_z >= 0) & (at_z < span_z)
    spots = place.shape[0]
    at_row = jnp.where(inside, at_x * span_y + at_y, -1)
    in_row = lax.broadcasted_iota(jnp.int32, (spots, rows), 1) == at_row
    in_row = in_row.astype(jnp.float32)
    in_lane = lax.broadcasted_iota(jnp.int32, (spots, span_z), 1) == at_z
    in_lane = in_lane.astype(jnp.float32)

    def misfit(field, column):
        lines = lax.dot_general(
            in_row, field, (((1,), (0,)), ((), ())), precision=HIGHEST,
            preferred_element_type=jnp.float32,
        )
        values = jnp.sum(lines * in_lane, axis=1, keepdims=True)
        mismatch = jnp.where(inside, values - targets_ref[:, column : column + 1], 0.0)
        return lax.dot_general(
            in_row, in_lane * mismatch, (((0,), (0,)), ((), ())), precision=HIGHEST,
            preferred_element_type=jnp.float32,
        )

    for load in loads[:2]:
        load.wait()
    ids = flat(ids_ref)
    walls = 0.5 * flat(wall_ref).astype(jnp.float32)
    table = jnp.broadcast_to(table_ref[...], (rows, 128))
    rate = jnp.concatenate(
        [
            jnp.take_along_axis(table, ids[:, i : i + 128], axis=1, mode="promise_in_bounds")
            for i in range(0, span_z, 128)
        ],
        axis=1,
    )
    inverse_loss = 1.0 / (1.0 + walls * rate)
    reflect = 2.0 * inverse_loss - 1.0

    for load in loads[2:]:
        load.wait()
    now = flat(now_ref)
    prior = flat(prior_ref)
    receive(NOW, now_in)
    two = inverse_loss * (2.0 * now + 0.25 * laplace(now, NOW)) - reflect * prior
    field_ref[TWO] = two.reshape(now_ref.shape)
    send(TWO, field_ref.at[TWO])
    incoming = flat(near_ref) + misfit(two, 0)

    receive(TWO, field_ref.at[TWO])
    three = inverse_loss * (2.0 * two + 0.25 * laplace(two, TWO)) - reflect * now
    adjoint_three = flat(end_ref) + misfit(three, 1)
    weighted_three = inverse_loss * adjoint_three
    field_ref[W3] = weighted_three.reshape(now_ref.shape)
    send(W3, field_ref.at[W3])
    term_three = weighted_three * (now - three)

    receive(W3, field_ref.at[W3])
    adjoint_two = incoming + 2.0 * weighted_three + 0.25 * laplace(weighted_three, W3)
    weighted_two = inverse_loss * adjoint_two
    field_ref[W2] = weighted_two.reshape(now_ref.shape)
    send(W2, field_ref.at[W2])

    terms = walls * (term_three + weighted_two * (prior - two))
    kinds = bins_ref.shape[0]

    @pl.loop(0, kinds, unroll=8)
    def _(kind):
        mine = jnp.where(ids == kind, terms, 0.0)
        mine = jnp.sum(mine.reshape(rows // 8, 8, span_z), axis=0)
        bins_ref[kind] = mine[:, :128] + mine[:, 128:]

    bins = jnp.sum(bins_ref[...], axis=1)
    ones = jnp.ones((8, 128), jnp.float32)
    sums = lax.dot_general(
        ones, bins, (((1,), (1,)), ((), ())), precision=HIGHEST,
        preferred_element_type=jnp.float32,
    )
    slots_ref[me] = jnp.concatenate([sums[:1], sums[:1]], axis=1)

    @pl.loop(1, count)
    def _(step):
        pltpu.make_async_remote_copy(
            src_ref=slots_ref.at[me],
            dst_ref=slots_ref.at[me],
            send_sem=sum_sems.at[0],
            recv_sem=sum_sems.at[1],
            device_id=peer(step),
            device_id_type=pl.DeviceIdType.MESH,
        ).start()

    result_ref[0] = (-reflect * adjoint_two).reshape(now_ref.shape)
    prior_copy = pltpu.make_async_copy(result_ref.at[0], prior_out, out_sems.at[0])
    prior_copy.start()

    receive(W2, field_ref.at[W2])
    result = -reflect * adjoint_three + 2.0 * weighted_two + 0.25 * laplace(weighted_two, W2)
    result_ref[1] = result.reshape(now_ref.shape)
    now_copy = pltpu.make_async_copy(result_ref.at[1], now_out, out_sems.at[1])
    now_copy.start()

    others = pltpu.make_async_remote_copy(
        src_ref=slots_ref.at[pl.ds(0, count - 1)],
        dst_ref=slots_ref.at[pl.ds(0, count - 1)],
        send_sem=sum_sems.at[0],
        recv_sem=sum_sems.at[1],
        device_id=peer(1),
        device_id_type=pl.DeviceIdType.MESH,
    )
    others.wait_recv()
    grad_out[...] = scaling * jnp.sum(slots_ref[...], axis=0)
    others.wait_send()
    sent(NOW, now_in)
    for level in (TWO, W3, W2):
        sent(level, field_ref.at[level])
    prior_copy.wait()
    now_copy.wait()


def local(
    sizes,
    pressure_prior,
    pressure_now,
    adjoint_end,
    adjoint_near,
    wall_faces,
    material_ids,
    admittance,
    receivers,
    targets,
):
    shape = pressure_now.shape
    span_x, span_y, span_z = shape
    count = math.prod(sizes)
    kinds = admittance.shape[0]
    scaling = 16.0 / math.sqrt(pressure_now.size * count)
    table = jnp.concatenate([admittance, admittance]).reshape(1, 2 * kinds)
    anywhere = pl.BlockSpec(memory_space=pl.ANY)
    in_vmem = pl.BlockSpec(memory_space=pltpu.VMEM)
    block = pltpu.VMEM(shape, jnp.float32)
    prior_out, now_out, grad = pl.pallas_call(
        functools.partial(kernel, sizes, scaling),
        out_shape=(
            jax.ShapeDtypeStruct(shape, jnp.float32),
            jax.ShapeDtypeStruct(shape, jnp.float32),
            jax.ShapeDtypeStruct((1, 128), jnp.float32),
        ),
        in_specs=[anywhere] * 6 + [in_vmem] * 3,
        out_specs=(anywhere, anywhere, in_vmem),
        scratch_shapes=[
            block,
            block,
            block,
            block,
            pltpu.VMEM(shape, jnp.int32),
            pltpu.VMEM(shape, jnp.int32),
            pltpu.VMEM((4,) + shape, jnp.float32),
            pltpu.VMEM((2,) + shape, jnp.float32),
            pltpu.VMEM((kinds, 8, 128), jnp.float32),
            pltpu.VMEM((count, 1, 128), jnp.float32),
            pltpu.VMEM((4, 2, span_y, span_z), jnp.float32),
            pltpu.VMEM((4, 2, span_x, 8, span_z), jnp.float32),
            pltpu.VMEM((4, span_x, span_y, span_z // 2), jnp.float32),
            pltpu.SemaphoreType.DMA((6,)),
            pltpu.SemaphoreType.DMA((2,)),
            pltpu.SemaphoreType.DMA((4, 5)),
            pltpu.SemaphoreType.DMA((4, 5)),
            pltpu.SemaphoreType.DMA((2,)),
        ],
        compiler_params=pltpu.CompilerParams(
            collective_id=0, has_side_effects=True, vmem_limit_bytes=32 * 1024 * 1024
        ),
    )(
        pressure_now,
        pressure_prior,
        adjoint_end,
        adjoint_near,
        wall_faces,
        material_ids,
        table,
        receivers,
        targets,
    )
    return prior_out, now_out, grad[0, :kinds]


def solution(mesh):
    cells = P(("rooms", "gx"), "gy", "gz")
    sizes = tuple(mesh.shape[axis] for axis in ("gx", "gy", "gz"))
    return jax.shard_map(
        functools.partial(local, sizes),
        mesh=mesh,
        in_specs=(cells,) * 6 + (P(), P("rooms", None), P("rooms", None)),
        out_specs=(cells, cells, P("rooms")),
        check_vma=False,
    )
```

time: 443 us -> 30.5 us (0.07)
  other arithmetic: 232 us -> 0.81 us
  local copies, waits for them, and re-layouts: 103 us -> 7.5 us
  starting transfers between devices: 65 us -> 0 us
  blocking collectives: 29.5 us -> 0 us
  Pallas kernels: 0 us -> 21.1 us
  waiting for transfers between devices: 11.2 us -> 0 us
    scatter-add x4 -> x0, other arithmetic: 229 us -> none  [the longest x2 227 us: per_material(): jax.ops.segment_sum(terms.reshape(-1), material_ids.reshape(-1), num_segm...]
    gather x4 -> x0, local copies, waits for them, and re-layouts: 98.8 us -> none  [the longest x2 97.2 us: local(): loss_rate = 0.5 * wall_count * admittance[material_ids]]
    ppermute x24 -> x0, starting transfers between devices: 65 us -> none  [the longest x12 49.5 us: padded_2(): lax.ppermute(tail, axis, [(i, (i + 1) % count) for i in range(ends)])]
    psum x1 -> x0, blocking collectives: 29.5 us -> none  [step_total(): lax.psum(per_material(terms, material_ids, kinds), ('gx', 'gy', 'gz'))]
    pallas_call x0 -> x1, Pallas kernels: none -> 21.1 us  [local(): pl.pallas_call(functools.partial(kernel, sizes, scaling), out_shape=(jax....]
    ppermute x24 -> x0, waiting for transfers between devices: 11.2 us -> none  [the longest x12 7.54 us: padded_2(): lax.ppermute(tail, axis, [(i, (i + 1) % count) for i in range(ends)])]
  transfers between devices with their start and end apart: 24 -> 0, of which waited for: 9 -> 0; matrix products, arithmetic and copies ran while one was open for 74% -> 0% of each run, Pallas kernels for 0% -> 0%
where the time goes in v1:
time: 30.5 us; the launch traced here: 30 us
  Pallas kernels  21.1 us (69%)
  local copies, waits for them, and re-layouts  7.5 us (25%)
  other arithmetic  0.81 us (3%)
  between operations  0.66 us (2%)
    pallas_call x1, Pallas kernels, local(): pl.pallas_call(functools.partial(kernel, sizes, scaling), out_shape=(jax....  21.1 us
    unnamed x16, local copies, waits for them, and re-layouts  6.99 us
    reshape x1, other arithmetic, local(): table = jnp.concatenate([admittance, admittance]).reshape(1, 2 * kinds)  0.81 us

profile of v1, /device:TPU:0, one launch (start us, length us, event | category | flops | bytes accessed | tf_op | source)
XLA Modules:
  0.0 30.0 jit_solution(6327887149486855124)
XLA Ops:
  0.6 0.0 copy-start
  0.6 0.8 %maximum_bitcast_fusion.table_ref = f32[1,128]{1,0:T(1,128)S(1)} fusion(f32[64]{0:T(128)} %param.15), kind=kLoop, calls=%fused_computation | loop fusion | flops 128 | bytes 768 | tf_op jit(solution)/shard_map/reshape | solution.py:321
  1.4 0.8 %copy.12.receivers_ref = s32[64,3]{1,0:T(8,128)S(1)} copy(s32[64,3]{0,1:T(4,128)} %param.16) | data formatting | bytes 1536 | tf_op args[7]
  2.2 0.8 %copy.13.targets_ref = f32[64,2]{1,0:T(8,128)S(1)} copy(f32[64,2]{0,1:T(2,128)} %param.17) | data formatting | bytes 1024 | tf_op args[8]
  3.0 0.0 copy-done
  3.0 0.0 copy-start.1
  3.0 0.8 %copy-done.1 = f32[2,32,256]{2,1,0:T(8,128)S(1)} copy-done((f32[2,32,256]{2,1,0:T(8,128)S(1)}, f32[2,32,256]{2,1,0:T(8,128)}, u32[]{:S(2)}) %copy-start.1) | copy-done | bytes 65560
  3.8 0.0 copy-start.2
  3.8 0.8 %copy-done.2 = f32[2,32,256]{2,1,0:T(8,128)S(1)} copy-done((f32[2,32,256]{2,1,0:T(8,128)S(1)}, f32[2,32,256]{2,1,0:T(8,128)}, u32[]{:S(2)}) %copy-start.2) | copy-done | bytes 65560
  4.7 0.0 copy-start.3
  4.7 0.8 %copy-done.3 = f32[2,32,256]{2,1,0:T(8,128)S(1)} copy-done((f32[2,32,256]{2,1,0:T(8,128)S(1)}, f32[2,32,256]{2,1,0:T(8,128)}, u32[]{:S(2)}) %copy-start.3) | copy-done | bytes 65560
  5.5 0.0 copy-start.4
  5.5 0.8 %copy-done.4 = s32[2,32,256]{2,1,0:T(8,128)S(1)} copy-done((s32[2,32,256]{2,1,0:T(8,128)S(1)}, s32[2,32,256]{2,1,0:T(8,128)}, u32[]{:S(2)}) %copy-start.4) | copy-done | bytes 65560
  6.3 0.0 copy-start.5
  6.3 0.8 %copy-done.5 = s32[2,32,256]{2,1,0:T(8,128)S(1)} copy-done((s32[2,32,256]{2,1,0:T(8,128)S(1)}, s32[2,32,256]{2,1,0:T(8,128)}, u32[]{:S(2)}) %copy-start.5) | copy-done | bytes 65560
  7.2 21.1 %shard_map.112 = (f32[2,32,256]{2,1,0:T(8,128)S(1)}, f32[2,32,256]{2,1,0:T(8,128)S(1)}, f32[1,128]{1,0:T(1,128)S(1)}) custom-call(f32[2,32,256]{2,1,0:T(8,128)S(1)} %copy-done, f32[2,32,256]{2,1,0:T(8,128)S(1)} %copy-done.1, f32[2,32,256]{2,1,0:T(8,128)S(1)} %copy-done.2, f32[2,32,256]{2,1,0:T(8,128)S(1)} %copy-done.3, s32[2,32,256]{2,1,0:T(8,128)S(1)} %copy-done.4, ...), custom_call_target="tpu_custom_call" | custom-call | tf_op jit(solution)/shard_map/pallas_call | solution.py:325
  28.3 0.5 %slice_bitcast_fusion = f32[64]{0:T(128)} fusion(f32[1,128]{1,0:T(1,128)S(1)} %get-tuple-element.8), kind=kLoop, calls=%fused_computation.1 | loop fusion | bytes 512 | tf_op jit(solution)/shard_map/squeeze | solution.py:368
  28.8 0.6 %copy.16 = f32[2,32,256]{2,1,0:T(8,128)} copy(f32[2,32,256]{2,1,0:T(8,128)S(1)} %get-tuple-element.12) | data formatting | bytes 131072
  29.4 0.6 %copy.17 = f32[2,32,256]{2,1,0:T(8,128)} copy(f32[2,32,256]{2,1,0:T(8,128)S(1)} %get-tuple-element.13) | data formatting | bytes 131072
Async XLA Ops:
  0.6 2.4 %copy-start = (f32[2,32,256]{2,1,0:T(8,128)S(1)}, f32[2,32,256]{2,1,0:T(8,128)}, u32[]{:S(2)}) copy-start(f32[2,32,256]{2,1,0:T(8,128)} %now_in.1) | copy-start | bytes 196612
  3.0 0.8 %copy-start.1 = (f32[2,32,256]{2,1,0:T(8,128)S(1)}, f32[2,32,256]{2,1,0:T(8,128)}, u32[]{:S(2)}) copy-start(f32[2,32,256]{2,1,0:T(8,128)} %prior_in.1) | copy-start | bytes 196612
  3.8 0.8 %copy-start.2 = (f32[2,32,256]{2,1,0:T(8,128)S(1)}, f32[2,32,256]{2,1,0:T(8,128)}, u32[]{:S(2)}) copy-start(f32[2,32,256]{2,1,0:T(8,128)} %end_in.1) | copy-start | bytes 196612
  4.7 0.8 %copy-start.3 = (f32[2,32,256]{2,1,0:T(8,128)S(1)}, f32[2,32,256]{2,1,0:T(8,128)}, u32[]{:S(2)}) copy-start(f32[2,32,256]{2,1,0:T(8,128)} %near_in.1) | copy-start | bytes 196612
  5.5 0.8 %copy-start.4 = (s32[2,32,256]{2,1,0:T(8,128)S(1)}, s32[2,32,256]{2,1,0:T(8,128)}, u32[]{:S(2)}) copy-start(s32[2,32,256]{2,1,0:T(8,128)} %wall_in.1) | copy-start | bytes 196612
  6.3 0.8 %copy-start.5 = (s32[2,32,256]{2,1,0:T(8,128)S(1)}, s32[2,32,256]{2,1,0:T(8,128)}, u32[]{:S(2)}) copy-start(s32[2,32,256]{2,1,0:T(8,128)} %ids_in.1) | copy-start | bytes 196612

commit v2 on v1

--- a/solution.py
+++ b/solution.py
@@ -8,6 +8,7 @@
 from jax.experimental.pallas import tpu as pltpu
 from jax.sharding import PartitionSpec as P
 
+VMEM_BYTES = 64 * 1024 * 1024
 HIGHEST = lax.Precision.HIGHEST
 NOW, TWO, W3, W2 = range(4)
 
@@ -182,35 +183,44 @@
         return ref[...].reshape(rows, span_z)
 
     place = receivers_ref[...]
-    at_x = place[:, 0:1] - ix * span_x
-    at_y = place[:, 1:2] - iy * span_y
-    at_z = place[:, 2:3] - iz * span_z
+    spots = place.shape[1]
+    at_x = place[0:1] - ix * span_x
+    at_y = place[1:2] - iy * span_y
+    at_z = place[2:3] - iz * span_z
     inside = (at_x >= 0) & (at_x < span_x) & (at_y >= 0) & (at_y < span_y)
     inside = inside & (at_z >= 0) & (at_z < span_z)
-    spots = place.shape[0]
     at_row = jnp.where(inside, at_x * span_y + at_y, -1)
-    in_row = lax.broadcasted_iota(jnp.int32, (spots, rows), 1) == at_row
+    in_row = lax.broadcasted_iota(jnp.int32, (rows, spots), 0) == at_row
     in_row = in_row.astype(jnp.float32)
-    in_lane = lax.broadcasted_iota(jnp.int32, (spots, span_z), 1) == at_z
-    in_lane = in_lane.astype(jnp.float32)
-
-    def misfit(field, column):
-        lines = lax.dot_general(
-            in_row, field, (((1,), (0,)), ((), ())), precision=HIGHEST,
+    in_lane = lax.broadcasted_iota(jnp.int32, (span_z, spots), 0) == at_z
+    in_lane = in_lane.astype(jnp.float32).astype(jnp.bfloat16)
+
+    def exact(values, pattern, dims):
+        parts = []
+        rest = values
+        for _ in range(3):
+            part = rest.astype(jnp.bfloat16)
+            rest = rest - part.astype(jnp.float32)
+            parts.append(part)
+        product = lax.dot_general(
+            jnp.concatenate(parts, axis=0), pattern, (dims, ((), ())),
             preferred_element_type=jnp.float32,
         )
-        values = jnp.sum(lines * in_lane, axis=1, keepdims=True)
-        mismatch = jnp.where(inside, values - targets_ref[:, column : column + 1], 0.0)
-        return lax.dot_general(
-            in_row, in_lane * mismatch, (((0,), (0,)), ((), ())), precision=HIGHEST,
-            preferred_element_type=jnp.float32,
-        )
+        high, middle, low = jnp.split(product, 3, axis=0)
+        return high + (middle + low)
+
+    def misfit(field, column):
+        lines = exact(field, in_lane, ((1,), (0,)))
+        values = jnp.sum(lines * in_row, axis=0, keepdims=True)
+        mismatch = jnp.where(inside, values - targets_ref[column : column + 1], 0.0)
+        return exact(in_row * mismatch, in_lane, ((1,), (1,)))
 
     for load in loads[:2]:
         load.wait()
     ids = flat(ids_ref)
     walls = 0.5 * flat(wall_ref).astype(jnp.float32)
-    table = jnp.broadcast_to(table_ref[...], (rows, 128))
+    table = table_ref[...]
+    table = jnp.broadcast_to(jnp.concatenate([table, table], axis=1), (rows, 128))
     rate = jnp.concatenate(
         [
             jnp.take_along_axis(table, ids[:, i : i + 128], axis=1, mode="promise_in_bounds")
@@ -292,13 +302,25 @@
         device_id_type=pl.DeviceIdType.MESH,
     )
     others.wait_recv()
-    grad_out[...] = scaling * jnp.sum(slots_ref[...], axis=0)
+    grad_out[...] = scaling * jnp.sum(slots_ref[...], axis=0)[:, : grad_out.shape[1]]
     others.wait_send()
     sent(NOW, now_in)
     for level in (TWO, W3, W2):
         sent(level, field_ref.at[level])
     prior_copy.wait()
     now_copy.wait()
+
+
+def write(prior_in, now_in, grad_in, prior_out, now_out, grad_out, sems):
+    copies = [
+        pltpu.make_async_copy(prior_in, prior_out, sems.at[0]),
+        pltpu.make_async_copy(now_in, now_out, sems.at[1]),
+        pltpu.make_async_copy(grad_in, grad_out, sems.at[2]),
+    ]
+    for copy in copies:
+        copy.start()
+    for copy in copies:
+        copy.wait()
 
 
 def local(
@@ -318,8 +340,7 @@
     count = math.prod(sizes)
     kinds = admittance.shape[0]
     scaling = 16.0 / math.sqrt(pressure_now.size * count)
-    table = jnp.concatenate([admittance, admittance]).reshape(1, 2 * kinds)
-    anywhere = pl.BlockSpec(memory_space=pl.ANY)
+    in_hbm = pl.BlockSpec(memory_space=pltpu.HBM)
     in_vmem = pl.BlockSpec(memory_space=pltpu.VMEM)
     block = pltpu.VMEM(shape, jnp.float32)
     prior_out, now_out, grad = pl.pallas_call(
@@ -327,10 +348,10 @@
         out_shape=(
             jax.ShapeDtypeStruct(shape, jnp.float32),
             jax.ShapeDtypeStruct(shape, jnp.float32),
-            jax.ShapeDtypeStruct((1, 128), jnp.float32),
+            jax.ShapeDtypeStruct((1, kinds), jnp.float32),
         ),
-        in_specs=[anywhere] * 6 + [in_vmem] * 3,
-        out_specs=(anywhere, anywhere, in_vmem),
+        in_specs=[in_hbm] * 6 + [in_vmem] * 3,
+        out_specs=(in_hbm, in_hbm, in_vmem),
         scratch_shapes=[
             block,
             block,
@@ -352,7 +373,7 @@
             pltpu.SemaphoreType.DMA((2,)),
         ],
         compiler_params=pltpu.CompilerParams(
-            collective_id=0, has_side_effects=True, vmem_limit_bytes=32 * 1024 * 1024
+            collective_id=0, has_side_effects=True, vmem_limit_bytes=VMEM_BYTES
         ),
     )(
         pressure_now,
@@ -361,11 +382,24 @@
         adjoint_near,
         wall_faces,
         material_ids,
-        table,
-        receivers,
-        targets,
+        admittance.reshape(1, kinds),
+        receivers.T,
+        targets.T,
     )
-    return prior_out, now_out, grad[0, :kinds]
+    results = (prior_out, now_out, grad)
+    prior_out, now_out, grad = pl.pallas_call(
+        write,
+        out_shape=(
+            jax.ShapeDtypeStruct(shape, jnp.float32),
+            jax.ShapeDtypeStruct(shape, jnp.float32),
+            jax.ShapeDtypeStruct((1, kinds), jnp.float32),
+        ),
+        in_specs=[in_hbm] * 3,
+        out_specs=(in_hbm,) * 3,
+        scratch_shapes=[pltpu.SemaphoreType.DMA((3,))],
+        compiler_params=pltpu.CompilerParams(vmem_limit_bytes=VMEM_BYTES),
+    )(*results)
+    return prior_out, now_out, grad.reshape(kinds)
 
 
 def solution(mesh):

time: 30.5 us -> 27.6 us (0.905)
  local copies, waits for them, and re-layouts: 7.5 us -> 0 us
  Pallas kernels: 21.1 us -> 26.8 us
  other arithmetic: 0.81 us -> 0 us
    unnamed x16 -> x0, local copies, waits for them, and re-layouts: 6.99 us -> none
    pallas_call x0 -> x1, Pallas kernels: none -> 5.12 us  [local(): pl.pallas_call(write, out_shape=(jax.ShapeDtypeStruct(shape, jnp.float32)...]
    reshape x1 -> x0, other arithmetic: 0.81 us -> none  [local(): table = jnp.concatenate([admittance, admittance]).reshape(1, 2 * kinds)]
    pallas_call x1, Pallas kernels: 21.1 us -> 21.7 us  [local(): pl.pallas_call(functools.partial(kernel, sizes, scaling), out_shape=(jax....]
    squeeze x1 -> x0, local copies, waits for them, and re-layouts: 0.51 us -> none  [local(): return (prior_out, now_out, grad[0, :kinds])]
where the time goes in v2:
time: 27.6 us; the launch traced here: 27.4 us
  Pallas kernels  26.8 us (97%)
  between operations  0.64 us (2%)
    pallas_call x1, Pallas kernels, local(): pl.pallas_call(functools.partial(kernel, sizes, scaling), out_shape=(jax....  21.7 us
    pallas_call x1, Pallas kernels, local(): pl.pallas_call(write, out_shape=(jax.ShapeDtypeStruct(shape, jnp.float32)...  5.12 us

profile of v2, /device:TPU:0, one launch (start us, length us, event | category | flops | bytes accessed | tf_op | source)
XLA Modules:
  0.0 27.4 jit_solution(18054464962208022642)
XLA Ops:
  0.6 21.7 %shard_map.112 = (f32[2,32,256]{2,1,0:T(8,128)}, f32[2,32,256]{2,1,0:T(8,128)}, f32[1,64]{1,0:T(1,128)}) custom-call(f32[2,32,256]{2,1,0:T(8,128)} %now_in.1, f32[2,32,256]{2,1,0:T(8,128)} %prior_in.1, f32[2,32,256]{2,1,0:T(8,128)} %end_in.1, f32[2,32,256]{2,1,0:T(8,128)} %near_in.1, s32[2,32,256]{2,1,0:T(8,128)} %wall_in.1, s32[2,32,256]{2,1,0:T(8,128)} %ids_in.1, ...), custom_call_target="tpu_custom_call" | custom-call | tf_op jit(solution)/shard_map/pallas_call | solution.py:346
  22.3 5.1 %shard_map.113 = (f32[2,32,256]{2,1,0:T(8,128)}, f32[2,32,256]{2,1,0:T(8,128)}, f32[1,64]{1,0:T(1,128)}) custom-call(f32[2,32,256]{2,1,0:T(8,128)} %get-tuple-element.9.prior_in, f32[2,32,256]{2,1,0:T(8,128)} %get-tuple-element.10.now_in, f32[1,64]{1,0:T(1,128)} %get-tuple-element.11.grad_in), custom_call_target="tpu_custom_call" | custom-call | tf_op jit(solution)/shard_map/pallas_call | solution.py:390

commit v3 on v2

--- a/solution.py
+++ b/solution.py
@@ -311,16 +311,10 @@
     now_copy.wait()
 
 
-def write(prior_in, now_in, grad_in, prior_out, now_out, grad_out, sems):
-    copies = [
-        pltpu.make_async_copy(prior_in, prior_out, sems.at[0]),
-        pltpu.make_async_copy(now_in, now_out, sems.at[1]),
-        pltpu.make_async_copy(grad_in, grad_out, sems.at[2]),
-    ]
-    for copy in copies:
-        copy.start()
-    for copy in copies:
-        copy.wait()
+def write(prior_in, now_in, grad_in, prior_out, now_out, grad_out):
+    prior_out[...] = prior_in[...]
+    now_out[...] = now_in[...]
+    grad_out[...] = grad_in[...]
 
 
 def local(
@@ -394,9 +388,8 @@
             jax.ShapeDtypeStruct(shape, jnp.float32),
             jax.ShapeDtypeStruct((1, kinds), jnp.float32),
         ),
-        in_specs=[in_hbm] * 3,
-        out_specs=(in_hbm,) * 3,
-        scratch_shapes=[pltpu.SemaphoreType.DMA((3,))],
+        in_specs=[in_vmem] * 3,
+        out_specs=(in_vmem,) * 3,
         compiler_params=pltpu.CompilerParams(vmem_limit_bytes=VMEM_BYTES),
     )(*results)
     return prior_out, now_out, grad.reshape(kinds)

time: 27.6 us -> 24 us (0.87)
  Pallas kernels: 26.8 us -> 23.2 us
    pallas_call x1, Pallas kernels: 5.12 us -> 1.53 us  [local(): pl.pallas_call(write, out_shape=(jax.ShapeDtypeStruct(shape, jnp.float32)...]
where the time goes in v3:
time: 24 us; the launch traced here: 23.8 us
  Pallas kernels  23.2 us (97%)
  between operations  0.64 us (3%)
    pallas_call x1, Pallas kernels, local(): pl.pallas_call(functools.partial(kernel, sizes, scaling), out_shape=(jax....  21.7 us
    pallas_call x1, Pallas kernels, local(): pl.pallas_call(write, out_shape=(jax.ShapeDtypeStruct(shape, jnp.float32)...  1.53 us

profile of v3, /device:TPU:0, one launch (start us, length us, event | category | flops | bytes accessed | tf_op | source)
XLA Modules:
  0.0 23.8 jit_solution(7193242204060649202)
XLA Ops:
  0.6 21.7 %shard_map.112 = (f32[2,32,256]{2,1,0:T(8,128)}, f32[2,32,256]{2,1,0:T(8,128)}, f32[1,64]{1,0:T(1,128)}) custom-call(f32[2,32,256]{2,1,0:T(8,128)} %now_in.1, f32[2,32,256]{2,1,0:T(8,128)} %prior_in.1, f32[2,32,256]{2,1,0:T(8,128)} %end_in.1, f32[2,32,256]{2,1,0:T(8,128)} %near_in.1, s32[2,32,256]{2,1,0:T(8,128)} %wall_in.1, s32[2,32,256]{2,1,0:T(8,128)} %ids_in.1, ...), custom_call_target="tpu_custom_call" | custom-call | tf_op jit(solution)/shard_map/pallas_call | solution.py:340
  22.3 1.5 %shard_map.113 = (f32[2,32,256]{2,1,0:T(8,128)}, f32[2,32,256]{2,1,0:T(8,128)}, f32[1,64]{1,0:T(1,128)}) custom-call(f32[2,32,256]{2,1,0:T(8,128)} %get-tuple-element.9.prior_in, f32[2,32,256]{2,1,0:T(8,128)} %get-tuple-element.10.now_in, f32[1,64]{1,0:T(1,128)} %get-tuple-element.11.grad_in), custom_call_target="tpu_custom_call" | custom-call | tf_op jit(solution)/shard_map/pallas_call | solution.py:384

commit v4 on v3

--- a/solution.py
+++ b/solution.py
@@ -10,7 +10,7 @@
 
 VMEM_BYTES = 64 * 1024 * 1024
 HIGHEST = lax.Precision.HIGHEST
-NOW, TWO, W3, W2 = range(4)
+PRIOR, LOSS, W3, W2 = range(4)
 
 
 def kernel(
@@ -41,11 +41,19 @@
     hx,
     hy,
     hz,
+    near_x,
+    near_y,
+    near_z,
+    near_xy,
+    near_xz,
+    near_yz,
     in_sems,
     out_sems,
     send_sems,
     recv_sems,
     sum_sems,
+    wide_send_sems,
+    wide_recv_sems,
 ):
     nx, ny, nz = sizes
     count = nx * ny * nz
@@ -76,9 +84,6 @@
             )
         )
     ]
-    for load in loads:
-        load.start()
-
     barrier = pltpu.get_barrier_semaphore()
 
     @pl.loop(1, count)
@@ -86,6 +91,9 @@
         pl.semaphore_signal(
             barrier, inc=1, device_id=peer(step), device_id_type=pl.DeviceIdType.MESH
         )
+
+    for load in loads:
+        load.start()
 
     pl.semaphore_wait(barrier, count - 1)
 
@@ -144,40 +152,178 @@
         for copy, sends, _ in links(level, source):
             when(sends, copy.wait_send)
 
-    send(NOW, now_in)
-
-    for test, buffer, side in (
-        (ix == 0, hx, 0),
-        (ix == nx - 1, hx, 1),
-        (iy == 0, hy, 0),
-        (iy == ny - 1, hy, 1),
-    ):
+    def wide_links(source):
+        sides_x = ((ix + 1, 0, span_x - 1, ix < nx - 1, ix > 0), (ix - 1, 1, 0, ix > 0, ix < nx - 1))
+        sides_y = (
+            (iy + 1, 0, pl.ds(span_y - 8, 8), iy < ny - 1, iy > 0),
+            (iy - 1, 1, pl.ds(0, 8), iy > 0, iy < ny - 1),
+        )
+        lanes = pl.ds(pl.multiple_of((1 - iz) * half, half), half)
+        other = 1 - iz
+        plan = []
+        for to_x, side, layer, sends, receives in sides_x:
+            plan.append((source, near_x.at[side], {"gx": to_x}, sends, receives))
+        for to_y, side, band, sends, receives in sides_y:
+            plan.append((source.at[:, band, :], near_y.at[side], {"gy": to_y}, sends, receives))
+        plan.append((source.at[:, :, lanes], near_z, {"gz": other}, None, None))
+        for to_x, side, layer, sends, receives in sides_x:
+            for to_y, side_y, band, sends_y, receives_y in sides_y:
+                plan.append(
+                    (
+                        source.at[layer, band, :],
+                        near_xy.at[side, side_y],
+                        {"gx": to_x, "gy": to_y},
+                        sends & sends_y,
+                        receives & receives_y,
+                    )
+                )
+            plan.append(
+                (
+                    source.at[layer, :, lanes],
+                    near_xz.at[side],
+                    {"gx": to_x, "gz": other},
+                    sends,
+                    receives,
+                )
+            )
+        for to_y, side, band, sends, receives in sides_y:
+            plan.append(
+                (
+                    source.at[:, band, lanes],
+                    near_yz.at[side],
+                    {"gy": to_y, "gz": other},
+                    sends,
+                    receives,
+                )
+            )
+        return [
+            (
+                pltpu.make_async_remote_copy(
+                    src_ref=part,
+                    dst_ref=target,
+                    send_sem=wide_send_sems.at[i],
+                    recv_sem=wide_recv_sems.at[i],
+                    device_id=where,
+                    device_id_type=pl.DeviceIdType.MESH,
+                ),
+                sends,
+                receives,
+            )
+            for i, (part, target, where, sends, receives) in enumerate(plan)
+        ]
+
+    for copy, sends, _ in wide_links(now_in):
+        when(sends, copy.start)
+    send(PRIOR, prior_in)
+
+    def clear(ref):
+        ref[...] = jnp.zeros(ref.shape, jnp.float32)
+
+    for side, test in ((0, ix == 0), (1, ix == nx - 1)):
 
         @pl.when(test)
         def _():
             for level in range(4):
-                buffer[level, side] = jnp.zeros(buffer.shape[2:], jnp.float32)
+                clear(hx.at[level, side])
+            for ref in (near_x, near_xy, near_xz):
+                clear(ref.at[side])
+
+    for side, test in ((0, iy == 0), (1, iy == ny - 1)):
+
+        @pl.when(test)
+        def _():
+            for level in range(4):
+                clear(hy.at[level, side])
+            clear(near_y.at[side])
+            clear(near_yz.at[side])
+
+    for side, test in ((0, ix == 0), (1, ix == nx - 1)):
+        for side_y, test_y in ((0, iy == 0), (1, iy == ny - 1)):
+
+            @pl.when(test_y & jnp.logical_not(test))
+            def _():
+                clear(near_xy.at[side, side_y])
 
     row = lax.broadcasted_iota(jnp.int32, (rows, span_z), 0)
     lane = lax.broadcasted_iota(jnp.int32, (rows, span_z), 1)
     top = lax.rem(row, span_y) == 0
     bottom = lax.rem(row, span_y) == span_y - 1
 
-    def laplace(field, level):
-        before_x = jnp.concatenate([hx[level, 0], field[: rows - span_y]], axis=0)
-        after_x = jnp.concatenate([field[span_y:], hx[level, 1]], axis=0)
-        shape = (span_x, span_y, span_z)
-        before_y = jnp.broadcast_to(hy[level, 0][:, 7:8, :], shape).reshape(rows, span_z)
-        after_y = jnp.broadcast_to(hy[level, 1][:, 0:1, :], shape).reshape(rows, span_z)
-        before_y = jnp.where(top, before_y, pltpu.roll(field, 1, 0))
-        after_y = jnp.where(bottom, after_y, pltpu.roll(field, rows - 1, 0))
-        beside = hz[level].reshape(rows, half)
-        before_z = jnp.where(iz == 1, beside[:, half - 1 :], 0.0)
-        after_z = jnp.where(iz == 0, beside[:, :1], 0.0)
-        before_z = jnp.where(lane == 0, before_z, pltpu.roll(field, 1, 1))
-        after_z = jnp.where(lane == span_z - 1, after_z, pltpu.roll(field, span_z - 1, 1))
-        total = before_x + after_x + before_y + after_y + before_z + after_z
-        return total - 6.0 * field
+    def across_y(field, before, after, first, last):
+        before = jnp.where(first, before, pltpu.roll(field, 1, 0))
+        return before + jnp.where(last, after, pltpu.roll(field, field.shape[0] - 1, 0))
+
+    def across_z(field, beside):
+        count_rows = field.shape[0]
+        before = jnp.where(iz == 1, beside[:, half - 1 :], 0.0)
+        after = jnp.where(iz == 0, beside[:, :1], 0.0)
+        lanes = lane[:count_rows]
+        before = jnp.where(lanes == 0, before, pltpu.roll(field, 1, 1))
+        return before + jnp.where(lanes == span_z - 1, after, pltpu.roll(field, span_z - 1, 1))
+
+    def spread(line, height):
+        layers, _, width = line.shape
+        shape = (layers, height, width)
+        return jnp.broadcast_to(line, shape).reshape(layers * height, width)
+
+    def laplace(field, x_0, x_1, y_0, y_1, z):
+        total = jnp.concatenate([x_0, field[: rows - span_y]], axis=0)
+        total = total + jnp.concatenate([field[span_y:], x_1], axis=0)
+        y_0, y_1 = spread(y_0[:, 7:8, :], span_y), spread(y_1[:, 0:1, :], span_y)
+        total = total + across_y(field, y_0, y_1, top, bottom)
+        return total + across_z(field, z) - 6.0 * field
+
+    def halo(level):
+        return (
+            hx[level, 0],
+            hx[level, 1],
+            hy[level, 0],
+            hy[level, 1],
+            hz[level].reshape(rows, half),
+        )
+
+    def step(field, laplacian, loss, earlier):
+        return loss * (2.0 * field + 0.25 * laplacian) - (2.0 * loss - 1.0) * earlier
+
+    def step_beside(now):
+        layers = []
+        for side, nearest in ((0, 1), (1, 0)):
+            centre = near_x[side, nearest]
+            own = now[:span_y] if side == 0 else now[rows - span_y :]
+            total = near_x[side, 1 - nearest] + own
+            total = total + across_y(
+                centre, near_xy[side, 0][7:8], near_xy[side, 1][0:1], top[:span_y], bottom[:span_y]
+            )
+            total = total + across_z(centre, near_xz[side]) - 6.0 * centre
+            layers.append(step(centre, total, hx[LOSS, side], hx[PRIOR, side]))
+        bands = []
+        for side in range(2):
+            height = span_x * 8
+            centre = near_y[side].reshape(height, span_z)
+            total = jnp.concatenate([near_xy[0, side], centre[: height - 8]], axis=0)
+            total = total + jnp.concatenate([centre[8:], near_xy[1, side]], axis=0)
+            if side == 0:
+                own = spread(now_ref[:, 0:1, :], 8)
+                total = total + pltpu.roll(centre, 1, 0) + own
+            else:
+                own = spread(now_ref[:, span_y - 1 : span_y, :], 8)
+                total = total + pltpu.roll(centre, height - 1, 0) + own
+            total = total + across_z(centre, near_yz[side].reshape(height, half)) - 6.0 * centre
+            loss = hy[LOSS, side].reshape(height, span_z)
+            earlier = hy[PRIOR, side].reshape(height, span_z)
+            bands.append(step(centre, total, loss, earlier).reshape(span_x, 8, span_z))
+        centre = near_z[...].reshape(rows, half)
+        total = jnp.concatenate([near_xz[0], centre[: rows - span_y]], axis=0)
+        total = total + jnp.concatenate([centre[span_y:], near_xz[1]], axis=0)
+        y_0 = spread(near_yz[0][:, 7:8, :], span_y)
+        y_1 = spread(near_yz[1][:, 0:1, :], span_y)
+        total = total + across_y(centre, y_0, y_1, top[:, :half], bottom[:, :half])
+        own = jnp.where(iz == 0, now[:, span_z - 1 :], now[:, :1])
+        inner = jnp.where(iz == 0, pltpu.roll(centre, half - 1, 1), pltpu.roll(centre, 1, 1))
+        total = total + inner + own - 6.0 * centre
+        loss = hz[LOSS].reshape(rows, half)
+        earlier = hz[PRIOR].reshape(rows, half)
+        return (*layers, *bands, step(centre, total, loss, earlier))
 
     def flat(ref):
         return ref[...].reshape(rows, span_z)
@@ -231,26 +377,33 @@
     inverse_loss = 1.0 / (1.0 + walls * rate)
     reflect = 2.0 * inverse_loss - 1.0
 
+    field_ref[LOSS] = inverse_loss.reshape(now_ref.shape)
+    send(LOSS, field_ref.at[LOSS])
+
     for load in loads[2:]:
         load.wait()
     now = flat(now_ref)
     prior = flat(prior_ref)
-    receive(NOW, now_in)
-    two = inverse_loss * (2.0 * now + 0.25 * laplace(now, NOW)) - reflect * prior
-    field_ref[TWO] = two.reshape(now_ref.shape)
-    send(TWO, field_ref.at[TWO])
-    incoming = flat(near_ref) + misfit(two, 0)
-
-    receive(TWO, field_ref.at[TWO])
-    three = inverse_loss * (2.0 * two + 0.25 * laplace(two, TWO)) - reflect * now
+    wide = wide_links(now_in)
+    for copy, _, receives in wide[:5]:
+        when(receives, copy.wait_recv)
+    around = (near_x[0, 1], near_x[1, 0], near_y[0], near_y[1], near_z[...].reshape(rows, half))
+    two = step(now, laplace(now, *around), inverse_loss, prior)
+    for copy, _, receives in wide[5:]:
+        when(receives, copy.wait_recv)
+
+    receive(PRIOR, prior_in)
+    receive(LOSS, field_ref.at[LOSS])
+    three = step(two, laplace(two, *step_beside(now)), inverse_loss, now)
     adjoint_three = flat(end_ref) + misfit(three, 1)
     weighted_three = inverse_loss * adjoint_three
     field_ref[W3] = weighted_three.reshape(now_ref.shape)
     send(W3, field_ref.at[W3])
     term_three = weighted_three * (now - three)
+    incoming = flat(near_ref) + misfit(two, 0)
 
     receive(W3, field_ref.at[W3])
-    adjoint_two = incoming + 2.0 * weighted_three + 0.25 * laplace(weighted_three, W3)
+    adjoint_two = incoming + 2.0 * weighted_three + 0.25 * laplace(weighted_three, *halo(W3))
     weighted_two = inverse_loss * adjoint_two
     field_ref[W2] = weighted_two.reshape(now_ref.shape)
     send(W2, field_ref.at[W2])
@@ -288,7 +441,7 @@
     prior_copy.start()
 
     receive(W2, field_ref.at[W2])
-    result = -reflect * adjoint_three + 2.0 * weighted_two + 0.25 * laplace(weighted_two, W2)
+    result = -reflect * adjoint_three + 2.0 * weighted_two + 0.25 * laplace(weighted_two, *halo(W2))
     result_ref[1] = result.reshape(now_ref.shape)
     now_copy = pltpu.make_async_copy(result_ref.at[1], now_out, out_sems.at[1])
     now_copy.start()
@@ -304,8 +457,10 @@
     others.wait_recv()
     grad_out[...] = scaling * jnp.sum(slots_ref[...], axis=0)[:, : grad_out.shape[1]]
     others.wait_send()
-    sent(NOW, now_in)
-    for level in (TWO, W3, W2):
+    for copy, sends, _ in wide_links(now_in):
+        when(sends, copy.wait_send)
+    sent(PRIOR, prior_in)
+    for level in (LOSS, W3, W2):
         sent(level, field_ref.at[level])
     prior_copy.wait()
     now_copy.wait()
@@ -360,11 +515,19 @@
             pltpu.VMEM((4, 2, span_y, span_z), jnp.float32),
             pltpu.VMEM((4, 2, span_x, 8, span_z), jnp.float32),
             pltpu.VMEM((4, span_x, span_y, span_z // 2), jnp.float32),
+            pltpu.VMEM((2,) + shape, jnp.float32),
+            pltpu.VMEM((2, span_x, 8, span_z), jnp.float32),
+            pltpu.VMEM((span_x, span_y, span_z // 2), jnp.float32),
+            pltpu.VMEM((2, 2, 8, span_z), jnp.float32),
+            pltpu.VMEM((2, span_y, span_z // 2), jnp.float32),
+            pltpu.VMEM((2, span_x, 8, span_z // 2), jnp.float32),
             pltpu.SemaphoreType.DMA((6,)),
             pltpu.SemaphoreType.DMA((2,)),
             pltpu.SemaphoreType.DMA((4, 5)),
             pltpu.SemaphoreType.DMA((4, 5)),
             pltpu.SemaphoreType.DMA((2,)),
+            pltpu.SemaphoreType.DMA((13,)),
+            pltpu.SemaphoreType.DMA((13,)),
         ],
         compiler_params=pltpu.CompilerParams(
             collective_id=0, has_side_effects=True, vmem_limit_bytes=VMEM_BYTES

time: 24 us -> 23.4 us (0.975)
  Pallas kernels: 23.2 us -> 22.6 us
    pallas_call x1, Pallas kernels: 21.7 us -> 21 us  [local(): pl.pallas_call(functools.partial(kernel, sizes, scaling), out_shape=(jax....]
where the time goes in v4:
time: 23.4 us; the launch traced here: 23.2 us
  Pallas kernels  22.6 us (97%)
  between operations  0.64 us (3%)
    pallas_call x1, Pallas kernels, local(): pl.pallas_call(functools.partial(kernel, sizes, scaling), out_shape=(jax....  21 us
    pallas_call x1, Pallas kernels, local(): pl.pallas_call(write, out_shape=(jax.ShapeDtypeStruct(shape, jnp.float32)...  1.53 us

profile of v4, /device:TPU:0, one launch (start us, length us, event | category | flops | bytes accessed | tf_op | source)
XLA Modules:
  0.0 23.2 jit_solution(5624879502131589950)
XLA Ops:
  0.6 21.0 %shard_map.112 = (f32[2,32,256]{2,1,0:T(8,128)}, f32[2,32,256]{2,1,0:T(8,128)}, f32[1,64]{1,0:T(1,128)}) custom-call(f32[2,32,256]{2,1,0:T(8,128)} %now_in.1, f32[2,32,256]{2,1,0:T(8,128)} %prior_in.1, f32[2,32,256]{2,1,0:T(8,128)} %end_in.1, f32[2,32,256]{2,1,0:T(8,128)} %near_in.1, s32[2,32,256]{2,1,0:T(8,128)} %wall_in.1, s32[2,32,256]{2,1,0:T(8,128)} %ids_in.1, ...), custom_call_target="tpu_custom_call" | custom-call | tf_op jit(solution)/shard_map/pallas_call | solution.py:495
  21.7 1.5 %shard_map.113 = (f32[2,32,256]{2,1,0:T(8,128)}, f32[2,32,256]{2,1,0:T(8,128)}, f32[1,64]{1,0:T(1,128)}) custom-call(f32[2,32,256]{2,1,0:T(8,128)} %get-tuple-element.9.prior_in, f32[2,32,256]{2,1,0:T(8,128)} %get-tuple-element.10.now_in, f32[1,64]{1,0:T(1,128)} %get-tuple-element.11.grad_in), custom_call_target="tpu_custom_call" | custom-call | tf_op jit(solution)/shard_map/pallas_call | solution.py:547

commit v5 on v4

--- a/solution.py
+++ b/solution.py
@@ -22,9 +22,9 @@
     near_in,
     wall_in,
     ids_in,
-    table_ref,
-    receivers_ref,
-    targets_ref,
+    table_in,
+    receivers_in,
+    targets_in,
     prior_out,
     now_out,
     grad_out,
@@ -34,8 +34,12 @@
     near_ref,
     wall_ref,
     ids_ref,
+    table_ref,
+    receivers_ref,
+    targets_ref,
     field_ref,
     result_ref,
+    grad_ref,
     bins_ref,
     slots_ref,
     hx,
@@ -77,6 +81,9 @@
             (
                 (ids_in, ids_ref),
                 (wall_in, wall_ref),
+                (table_in, table_ref),
+                (receivers_in, receivers_ref),
+                (targets_in, targets_ref),
                 (now_in, now_ref),
                 (prior_in, prior_ref),
                 (end_in, end_ref),
@@ -328,6 +335,9 @@
     def flat(ref):
         return ref[...].reshape(rows, span_z)
 
+    for load in loads[:5]:
+        load.wait()
+
     place = receivers_ref[...]
     spots = place.shape[1]
     at_x = place[0:1] - ix * span_x
@@ -361,8 +371,6 @@
         mismatch = jnp.where(inside, values - targets_ref[column : column + 1], 0.0)
         return exact(in_row * mismatch, in_lane, ((1,), (1,)))
 
-    for load in loads[:2]:
-        load.wait()
     ids = flat(ids_ref)
     walls = 0.5 * flat(wall_ref).astype(jnp.float32)
     table = table_ref[...]
@@ -380,7 +388,7 @@
     field_ref[LOSS] = inverse_loss.reshape(now_ref.shape)
     send(LOSS, field_ref.at[LOSS])
 
-    for load in loads[2:]:
+    for load in loads[5:]:
         load.wait()
     now = flat(now_ref)
     prior = flat(prior_ref)
@@ -455,7 +463,9 @@
         device_id_type=pl.DeviceIdType.MESH,
     )
     others.wait_recv()
-    grad_out[...] = scaling * jnp.sum(slots_ref[...], axis=0)[:, : grad_out.shape[1]]
+    grad_ref[...] = scaling * jnp.sum(slots_ref[...], axis=0)[:, : grad_ref.shape[1]]
+    grad_copy = pltpu.make_async_copy(grad_ref, grad_out, out_sems.at[2])
+    grad_copy.start()
     others.wait_send()
     for copy, sends, _ in wide_links(now_in):
         when(sends, copy.wait_send)
@@ -464,6 +474,7 @@
         sent(level, field_ref.at[level])
     prior_copy.wait()
     now_copy.wait()
+    grad_copy.wait()
 
 
 def write(prior_in, now_in, grad_in, prior_out, now_out, grad_out):
@@ -499,8 +510,8 @@
             jax.ShapeDtypeStruct(shape, jnp.float32),
             jax.ShapeDtypeStruct((1, kinds), jnp.float32),
         ),
-        in_specs=[in_hbm] * 6 + [in_vmem] * 3,
-        out_specs=(in_hbm, in_hbm, in_vmem),
+        in_specs=[in_hbm] * 9,
+        out_specs=(in_hbm,) * 3,
         scratch_shapes=[
             block,
             block,
@@ -508,8 +519,12 @@
             block,
             pltpu.VMEM(shape, jnp.int32),
             pltpu.VMEM(shape, jnp.int32),
+            pltpu.VMEM((1, kinds), jnp.float32),
+            pltpu.VMEM(receivers.shape[::-1], jnp.int32),
+            pltpu.VMEM(targets.shape[::-1], jnp.float32),
             pltpu.VMEM((4,) + shape, jnp.float32),
             pltpu.VMEM((2,) + shape, jnp.float32),
+            pltpu.VMEM((1, kinds), jnp.float32),
             pltpu.VMEM((kinds, 8, 128), jnp.float32),
             pltpu.VMEM((count, 1, 128), jnp.float32),
             pltpu.VMEM((4, 2, span_y, span_z), jnp.float32),
@@ -521,8 +536,8 @@
             pltpu.VMEM((2, 2, 8, span_z), jnp.float32),
             pltpu.VMEM((2, span_y, span_z // 2), jnp.float32),
             pltpu.VMEM((2, span_x, 8, span_z // 2), jnp.float32),
-            pltpu.SemaphoreType.DMA((6,)),
-            pltpu.SemaphoreType.DMA((2,)),
+            pltpu.SemaphoreType.DMA((9,)),
+            pltpu.SemaphoreType.DMA((3,)),
             pltpu.SemaphoreType.DMA((4, 5)),
             pltpu.SemaphoreType.DMA((4, 5)),
             pltpu.SemaphoreType.DMA((2,)),

time: 23.4 us -> 22.9 us (0.979)
  Pallas kernels: 22.6 us -> 22.1 us
    pallas_call x1, Pallas kernels: 21 us -> 20.6 us  [local(): pl.pallas_call(functools.partial(kernel, sizes, scaling), out_shape=(jax....]
where the time goes in v5:
time: 22.9 us; the launch traced here: 22.7 us
  Pallas kernels  22.1 us (97%)
  between operations  0.64 us (3%)
    pallas_call x1, Pallas kernels, local(): pl.pallas_call(functools.partial(kernel, sizes, scaling), out_shape=(jax....  20.6 us
    pallas_call x1, Pallas kernels, local(): pl.pallas_call(write, out_shape=(jax.ShapeDtypeStruct(shape, jnp.float32)...  1.53 us

profile of v5, /device:TPU:0, one launch (start us, length us, event | category | flops | bytes accessed | tf_op | source)
XLA Modules:
  0.0 22.7 jit_solution(614435258703186897)
XLA Ops:
  0.6 20.6 %shard_map.112 = (f32[2,32,256]{2,1,0:T(8,128)}, f32[2,32,256]{2,1,0:T(8,128)}, f32[1,64]{1,0:T(1,128)}) custom-call(f32[2,32,256]{2,1,0:T(8,128)} %now_in.1, f32[2,32,256]{2,1,0:T(8,128)} %prior_in.1, f32[2,32,256]{2,1,0:T(8,128)} %end_in.1, f32[2,32,256]{2,1,0:T(8,128)} %near_in.1, s32[2,32,256]{2,1,0:T(8,128)} %wall_in.1, s32[2,32,256]{2,1,0:T(8,128)} %ids_in.1, ...), custom_call_target="tpu_custom_call" | custom-call | tf_op jit(solution)/shard_map/pallas_call | solution.py:506
  21.2 1.5 %shard_map.113 = (f32[2,32,256]{2,1,0:T(8,128)}, f32[2,32,256]{2,1,0:T(8,128)}, f32[1,64]{1,0:T(1,128)}) custom-call(f32[2,32,256]{2,1,0:T(8,128)} %get-tuple-element.9.prior_in, f32[2,32,256]{2,1,0:T(8,128)} %get-tuple-element.10.now_in, f32[1,64]{1,0:T(1,128)} %get-tuple-element.11.grad_in), custom_call_target="tpu_custom_call" | custom-call | tf_op jit(solution)/shard_map/pallas_call | solution.py:562
